TPU v7x, 32 devices: a whole 2x2x4 slice. The times are simulated.
32 devices in a mesh: ctx: 8 (over y, x, core), section: 4 (over z).
Axes of the slice: x: 2, y: 2, z: 4, core: 2. Of those that a mesh axis runs over, the one named last changes fastest.
Arguments:
- queries: bfloat16 [4, 1024, 4096], P('section', 'ctx'), may hold values from -24 to 24
- keys: bfloat16 [4, 1024, 512], P('section', 'ctx'), may hold values from -24 to 24
- values: bfloat16 [4, 1024, 512], P('section', 'ctx'), may hold values from -6 to 6
- doc_lengths: int32 [4, 4], P('section'), may hold values from 1 to 512, 1024 in all within a row
- interp_num: int32 [1], replicated, may hold values from 250 to 999
- interp_den: int32 [1], replicated, may hold values from 1000 to 1999
Outputs:
- handed: bfloat16 [4, 1024, 4096], P('section', 'ctx')
Inputs may be any that keep to these rules, and one draw needn't show every extreme that they name: `doc_lengths`: each row sums to 1024; its longest document has exactly 512 tokens.
All inputs are finite; a program needn't handle non-finite values.
Results may differ from a plain program's by a relative error of at most 0.0099.
Values may be sent and summed in bfloat16 or wider, within the bound.
A program may use at most 64 MiB of HBM per device.

v0:
```python
from functools import partial
import math

import jax
import jax.numpy as jnp
from jax import lax
from jax.sharding import PartitionSpec as P

QUERY_HEADS = 32
KEY_VALUE_HEADS = 4
HEAD_DIMENSION = 128


THETA = 500000.0
document_masked_scores = -1e30


def passed_along(block, axis, distance):
    devices = range(lax.axis_size(axis))
    route = [((i - distance) % len(devices), i) for i in devices]
    return lax.ppermute(block, axis, route)


def document_info(positions, lengths):
    doc_ends = jnp.cumsum(lengths)
    passed = positions[:, None] >= doc_ends[None, :]
    doc_ids = jnp.sum(passed.astype(jnp.int32), axis=1)
    starts = jnp.sum(jnp.where(passed, lengths[None, :], 0), axis=1)
    return (doc_ids, positions - starts)


def rotation_tables(input_array, position_starts, stretch_factor):
    half_size = HEAD_DIMENSION // 2
    inverse_freq = THETA ** (-(2.0 * jnp.arange(half_size, dtype=jnp.float32)) / HEAD_DIMENSION)
    angles = position_starts.astype(jnp.float32)[:, None] * stretch_factor * inverse_freq[None, :]
    cosine = jnp.cos(angles)[:, None, :]
    sine = jnp.sin(angles)[:, None, :]
    widened = input_array.astype(jnp.float32)
    first_half = widened[..., :half_size]
    second_half = widened[..., half_size:]
    joined = jnp.concatenate(
        [first_half * cosine - second_half * sine, second_half * cosine + first_half * sine],
        axis=-1,
    )
    return joined.astype(jnp.bfloat16)


def absorb(state, query_part, query_pos, query_docs, key_part, value_part, key_positions, key_docs):
    run_max, run_total, run_sum = state
    scores = jnp.einsum(
        "qhgd,khd->qhgk", query_part, key_part, preferred_element_type=jnp.float32
    ) * (1.0 / math.sqrt(HEAD_DIMENSION))
    allowed = (key_positions[None, :] <= query_pos[:, None]) & (
        key_docs[None, :] == query_docs[:, None]
    )
    allowed_full = allowed[:, None, None, :]
    scores = jnp.where(allowed_full, scores, document_masked_scores)
    new_max = jnp.maximum(run_max, jnp.max(scores, axis=-1))
    rescale = jnp.exp(run_max - new_max)
    weights = jnp.where(allowed_full, jnp.exp(scores - new_max[..., None]), 0.0)
    run_total = run_total * rescale + jnp.sum(weights, axis=-1)
    run_sum = run_sum * rescale[..., None] + jnp.einsum(
        "qhgk,khd->qhgd",
        weights.astype(jnp.bfloat16),
        value_part,
        preferred_element_type=jnp.float32,
    )
    return (new_max, run_total, run_sum)


def keep_state(state):
    return state


def on_device(queries, keys, values, doc_lengths, interp_num, interp_den):
    rows_of_tokens = queries.shape[1]
    rows_per_half = rows_of_tokens // 2
    ctx_count = lax.axis_size("ctx")
    shard_index = lax.axis_index("ctx")
    query_group_width = QUERY_HEADS // KEY_VALUE_HEADS
    stretch_factor = interp_num[0].astype(jnp.float32) / interp_den[0].astype(jnp.float32)
    lengths = doc_lengths[0]
    local_rows = jnp.arange(rows_of_tokens, dtype=jnp.int32)
    positions = jnp.where(
        local_rows < rows_per_half,
        shard_index * rows_per_half + local_rows,
        (2 * ctx_count - 1 - shard_index) * rows_per_half + local_rows - rows_per_half,
    )
    doc_ids, position_starts = document_info(positions, lengths)
    turned_queries = rotation_tables(
        queries[0].reshape(rows_of_tokens, QUERY_HEADS, HEAD_DIMENSION),
        position_starts,
        stretch_factor,
    ).reshape(rows_of_tokens, KEY_VALUE_HEADS, query_group_width, HEAD_DIMENSION)
    turned_keys = rotation_tables(
        keys[0].reshape(rows_of_tokens, KEY_VALUE_HEADS, HEAD_DIMENSION),
        position_starts,
        stretch_factor,
    ).reshape(rows_of_tokens, KEY_VALUE_HEADS * HEAD_DIMENSION)
    value_rows = values[0]
    query_parts = (
        (turned_queries[:rows_per_half], positions[:rows_per_half], doc_ids[:rows_per_half]),
        (turned_queries[rows_per_half:], positions[rows_per_half:], doc_ids[rows_per_half:]),
    )

    def absorb_block(carry, current_key_block, current_value_block, first_shard, number_of_shards):
        reshaped_keys = current_key_block.reshape(
            number_of_shards, 2, rows_per_half, KEY_VALUE_HEADS, HEAD_DIMENSION
        )
        reshaped_values = current_value_block.reshape(
            number_of_shards, 2, rows_per_half, KEY_VALUE_HEADS, HEAD_DIMENSION
        )
        shard_ids = first_shard + jnp.arange(number_of_shards, dtype=jnp.int32)
        within = jnp.arange(rows_per_half, dtype=jnp.int32)
        early_pos = (shard_ids[:, None] * rows_per_half + within[None, :]).reshape(-1)
        late_pos = (
            (2 * ctx_count - 1 - shard_ids)[:, None] * rows_per_half + within[None, :]
        ).reshape(-1)
        states = list(carry)
        for neighbor_index, key_positions in ((0, early_pos), (1, late_pos)):
            key_docs, unused = document_info(key_positions, lengths)
            neighbor_keys = reshaped_keys[:, neighbor_index].reshape(
                number_of_shards * rows_per_half, KEY_VALUE_HEADS, HEAD_DIMENSION
            )
            neighbor_values = reshaped_values[:, neighbor_index].reshape(
                number_of_shards * rows_per_half, KEY_VALUE_HEADS, HEAD_DIMENSION
            )
            for half_number in range(2):
                part_rows, part_pos, part_docs = query_parts[half_number]
                needed = jnp.min(key_positions) <= jnp.max(part_pos)
                update = partial(
                    absorb,
                    query_part=part_rows,
                    query_pos=part_pos,
                    query_docs=part_docs,
                    key_part=neighbor_keys,
                    value_part=neighbor_values,
                    key_positions=key_positions,
                    key_docs=key_docs,
                )
                states[half_number] = lax.cond(needed, update, keep_state, states[half_number])
        return tuple(states)

    start_state = (
        jnp.full(
            (rows_per_half, KEY_VALUE_HEADS, query_group_width), document_masked_scores, jnp.float32
        ),
        jnp.zeros((rows_per_half, KEY_VALUE_HEADS, query_group_width), jnp.float32),
        jnp.zeros((rows_per_half, KEY_VALUE_HEADS, query_group_width, HEAD_DIMENSION), jnp.float32),
    )
    initial = (start_state, start_state)
    key_fragment = lax.all_gather(turned_keys, "ctx", axis=0, tiled=True)
    value_fragment = lax.all_gather(value_rows, "ctx", axis=0, tiled=True)
    number_of_shards = key_fragment.shape[0] // rows_of_tokens
    limit = max(1, 512 // rows_of_tokens)
    sharded_blocks = max(
        (
            divisor
            for divisor in range(1, min(number_of_shards, limit) + 1)
            if number_of_shards % divisor == 0
        )
    )
    number_of_blocks = number_of_shards // sharded_blocks
    first_shard = jnp.int32(0) // rows_of_tokens
    key_block_list = key_fragment.reshape(
        number_of_blocks, sharded_blocks * rows_of_tokens, KEY_VALUE_HEADS * HEAD_DIMENSION
    )
    value_block_list = value_fragment.reshape(
        number_of_blocks, sharded_blocks * rows_of_tokens, KEY_VALUE_HEADS * HEAD_DIMENSION
    )

    def one_block(state, inputs):
        current_key_block, current_value_block, block_number = inputs
        return (
            absorb_block(
                state,
                current_key_block,
                current_value_block,
                block_number * sharded_blocks,
                sharded_blocks,
            ),
            None,
        )

    result, unused = lax.scan(
        one_block,
        initial,
        (key_block_list, value_block_list, jnp.arange(number_of_blocks, dtype=jnp.int32)),
    )
    finished = [state[2] / state[1][..., None] for state in result]
    attended = (
        jnp.concatenate(finished, axis=0)
        .reshape(rows_of_tokens, QUERY_HEADS * HEAD_DIMENSION)
        .astype(jnp.bfloat16)
    )
    return passed_along(attended[None], "section", 1)


def solution(mesh):
    placed = (
        P("section", "ctx", None),
        P("section", "ctx", None),
        P("section", "ctx", None),
        P("section", None),
        P(),
        P(),
    )
    return jax.shard_map(
        on_device, mesh=mesh, in_specs=placed, out_specs=P("section", "ctx", None), check_vma=False
    )
```

profile of v0, /device:TPU:0, one launch (start us, length us, event | category | flops | bytes accessed | tf_op | source)
XLA Modules:
  0.0 179.5 jit_solution(10480818396437773528)
XLA Ops:
  14.9 2.4 %add_convert_fusion = (bf16[128,32,64]{2,0,1:T(8,128)(2,1)S(1)}, bf16[128,32,64]{2,0,1:T(8,128)(2,1)S(1)}) fusion(f32[128,32,64]{2,1,0:T(8,128)S(1)} %get-tuple-element.544, f32[128,32,64]{2,1,0:T(8,128)S(1)} %get-tuple-element.543, f32[128,64]{1,0:T(8,128)S(1)} %get-tuple-element.548, f32[128,64]{1,0:T(8,128)S(1)} %get-tuple-element.547), kind=kLoop, calls=%fused_computation.68 | loop fusion | flops 2097152 | bytes 3211264 | tf_op jit(solution)/shard_map/convert.5
  17.3 1.6 pad_maximum_fusion.1
  18.9 1.3 slice_reduce_fusion
  20.2 18.2 %all-gather.4.cloned.1.call-done = bf16[1024,512]{1,0:T(8,128)(2,1)} async-done(((bf16[128,512]{1,0:T(8,128)(2,1)}), bf16[1024,512]{1,0:T(8,128)(2,1)}) %all-gather.4.cloned.1.call-update) | async-done | bytes 1048592 | tf_op jit(solution)/shard_map/all_gather | solution.py:152
  38.4 25.4 %all-gather.6.cloned.1.call-done = bf16[1,1024,512]{2,1,0:T(8,128)(2,1)} async-done(((bf16[1,128,512]{2,1,0:T(8,128)(2,1)}), bf16[1,1024,512]{2,1,0:T(8,128)(2,1)}) %all-gather.6.cloned.1.call-update) | async-done | bytes 1048592 | tf_op jit(solution)/shard_map/all_gather | solution.py:153
  66.3 75.0 %while.22 = (s32[]{:T(128)}, f32[64,4,8]{0,2,1:T(8,128)S(1)}, f32[64,4,8]{0,2,1:T(8,128)}, f32[64,4,8,128]{3,2,0,1:T(8,128)S(1)}, f32[64,4,8]{0,2,1:T(8,128)}, /...) while((s32[]{:T(128)}, f32[64,4,8]{0,2,1:T(8,128)S(1)}, ...), condition=%wide.region_27.28_spmd, body=%wide.region_6.27_spmd.sunk | while | flops 1094932992 | bytes 46277912 | solution.py:185
  69.9 1.3 convert_reduce_fusion.3
  73.5 1.9 %fusion.48 = (bf16[4,1,64,4,128]{4,3,2,1,0:T(4,128)(2,1)S(1)}, bf16[4,1,64,4,128]{4,3,2,1,0:T(4,128)(2,1)}) fusion(bf16[4,2,64,4,128]{4,3,2,1,0:T(4,128)(2,1)} %reshape.436), kind=kLoop, calls=%fused_computation.93.clone.1 | loop fusion | bytes 1048576 | tf_op jit(solution)/shard_map/while/body/eval_jaxpr/slice | solution.py:122
  77.7 8.8 %conditional.10 = ((f32[64,4,8]{0,2,1:T(8,128)}, f32[64,4,8]{0,2,1:T(8,128)}, f32[64,4,8,128]{3,2,0,1:T(8,128)S(1)})) conditional(s32[]{:T(128)} %convert_element_type.122, (f32[64,4,8]{0,2,1:T(8,128)}, f32[64,4,8]{0,2,1:T(8,128)}, f32[64,4,8,128]{3,2,0,1:T(8,128)S(1)}) %tuple.113, (s32[4,64]{1,0:T(4,128)S(1)}, s32[64]{0:T(128)}, ...), branch_computations={%region_19.19_spmd, %region_20.22_spmd} | conditional | flops 273731584 | bytes 9695832 | solution.py:141
  78.6 1.7 fusion.16
  81.9 1.4 multiply_add_fusion.2
  84.1 1.8 %fusion.19 = f32[64,4,8,128]{3,2,0,1:T(8,128)S(1)} fusion(bf16[64,4,8,256]{3,0,2,1:T(8,128)(2,1)S(1)} %get-tuple-element.519, f32[64,4,8,128]{3,2,0,1:T(8,128)S(1)} %get-tuple-element.327, f32[64,4,8]{2,0,1:T(8,128)S(1)} %copy.45, bf16[256,4,128,1]{2,1,0,3:T(4,128)(2,1)} %bitcast.115), kind=kOutput, calls=%fused_computation.34 | convolution fusion | flops 134742016 | bytes 3416064 | tf_op jit(solution)/shard_map/while/body/eval_jaxpr/cond/branch_1_fun/qhgk,khd->qhgd/dot_general | solution.py:62
  87.9 9.4 %conditional.11 = ((f32[64,4,8]{0,2,1:T(8,128)}, f32[64,4,8]{0,2,1:T(8,128)}, f32[64,4,8,128]{3,2,0,1:T(8,128)S(1)})) conditional(s32[]{:T(128)} %convert_element_type.121, (f32[64,4,8]{0,2,1:T(8,128)}, f32[64,4,8]{0,2,1:T(8,128)}, f32[64,4,8,128]{3,2,0,1:T(8,128)S(1)}) %get-tuple-element.811, (s32[4,64]{1,0:T(4,128)}, s32[64]{0:T(128)}, ...), branch_computations={%region_23.23_spmd, %region_24.26_spmd} | conditional | flops 273731584 | bytes 9695832 | solution.py:141
  89.4 1.6 fusion.24
  92.6 1.4 multiply_add_fusion.3
  94.8 1.8 %fusion.27 = f32[64,4,8,128]{3,2,0,1:T(8,128)S(1)} fusion(bf16[64,4,8,256]{3,0,2,1:T(8,128)(2,1)S(1)} %get-tuple-element.523, f32[64,4,8,128]{3,2,0,1:T(8,128)S(1)} %get-tuple-element.337, f32[64,4,8]{2,0,1:T(8,128)S(1)} %copy.47, bf16[256,4,128,1]{2,1,0,3:T(4,128)(2,1)} %bitcast.111), kind=kOutput, calls=%fused_computation.48 | convolution fusion | flops 134742016 | bytes 3416064 | tf_op jit(solution)/shard_map/while/body/eval_jaxpr/cond/branch_1_fun/qhgk,khd->qhgd/dot_general | solution.py:62
  98.4 8.1 %conditional.8 = ((f32[64,4,8]{0,2,1:T(8,128)S(1)}, f32[64,4,8]{0,2,1:T(8,128)}, f32[64,4,8,128]{3,2,0,1:T(8,128)S(1)})) conditional(s32[]{:T(128)} %convert_element_type.120, (f32[64,4,8]{0,2,1:T(8,128)S(1)}, f32[64,4,8]{0,2,1:T(8,128)}, f32[64,4,8,128]{3,2,0,1:T(8,128)S(1)}) %tuple.110, (s32[4,64]{1,0:T(4,128)}, s32[64]{0:T(128)}, ...), branch_computations={%region_10.10_spmd, %region_11.13_spmd} | conditional | flops 273731584 | bytes 9761424 | solution.py:141
  100.0 1.7 fusion
  104.6 1.8 %fusion.3 = f32[64,4,8,128]{3,2,0,1:T(8,128)S(1)} fusion(bf16[64,4,8,256]{3,0,2,1:T(8,128)(2,1)S(1)} %get-tuple-element.511, f32[64,4,8,128]{3,2,0,1:T(8,128)S(1)} %get-tuple-element.307, f32[64,4,8]{2,0,1:T(8,128)S(1)} %copy.41, bf16[256,4,128,1]{2,1,0,3:T(4,128)(2,1)} %bitcast.116), kind=kOutput, calls=%fused_computation.6 | convolution fusion | flops 134742016 | bytes 3416064 | tf_op jit(solution)/shard_map/while/body/eval_jaxpr/cond/branch_1_fun/qhgk,khd->qhgd/dot_general | solution.py:62
  107.9 1.3 dynamic_slice.22
  111.5 1.3 convert_reduce_fusion.3
  115.0 1.9 %fusion.48 = (bf16[4,1,64,4,128]{4,3,2,1,0:T(4,128)(2,1)S(1)}, bf16[4,1,64,4,128]{4,3,2,1,0:T(4,128)(2,1)}) fusion(bf16[4,2,64,4,128]{4,3,2,1,0:T(4,128)(2,1)} %reshape.436), kind=kLoop, calls=%fused_computation.93.clone.1 | loop fusion | bytes 1048576 | tf_op jit(solution)/shard_map/while/body/eval_jaxpr/slice | solution.py:122
  119.3 8.8 %conditional.10 = ((f32[64,4,8]{0,2,1:T(8,128)}, f32[64,4,8]{0,2,1:T(8,128)}, f32[64,4,8,128]{3,2,0,1:T(8,128)S(1)})) conditional(s32[]{:T(128)} %convert_element_type.122, (f32[64,4,8]{0,2,1:T(8,128)}, f32[64,4,8]{0,2,1:T(8,128)}, f32[64,4,8,128]{3,2,0,1:T(8,128)S(1)}) %tuple.113, (s32[4,64]{1,0:T(4,128)S(1)}, s32[64]{0:T(128)}, ...), branch_computations={%region_19.19_spmd, %region_20.22_spmd} | conditional | flops 273731584 | bytes 9695832 | solution.py:141
  120.2 1.7 fusion.16
  123.4 1.4 multiply_add_fusion.2
  125.6 1.8 %fusion.19 = f32[64,4,8,128]{3,2,0,1:T(8,128)S(1)} fusion(bf16[64,4,8,256]{3,0,2,1:T(8,128)(2,1)S(1)} %get-tuple-element.519, f32[64,4,8,128]{3,2,0,1:T(8,128)S(1)} %get-tuple-element.327, f32[64,4,8]{2,0,1:T(8,128)S(1)} %copy.45, bf16[256,4,128,1]{2,1,0,3:T(4,128)(2,1)} %bitcast.115), kind=kOutput, calls=%fused_computation.34 | convolution fusion | flops 134742016 | bytes 3416064 | tf_op jit(solution)/shard_map/while/body/eval_jaxpr/cond/branch_1_fun/qhgk,khd->qhgd/dot_general | solution.py:62
  129.4 9.4 %conditional.11 = ((f32[64,4,8]{0,2,1:T(8,128)}, f32[64,4,8]{0,2,1:T(8,128)}, f32[64,4,8,128]{3,2,0,1:T(8,128)S(1)})) conditional(s32[]{:T(128)} %convert_element_type.121, (f32[64,4,8]{0,2,1:T(8,128)}, f32[64,4,8]{0,2,1:T(8,128)}, f32[64,4,8,128]{3,2,0,1:T(8,128)S(1)}) %get-tuple-element.811, (s32[4,64]{1,0:T(4,128)}, s32[64]{0:T(128)}, ...), branch_computations={%region_23.23_spmd, %region_24.26_spmd} | conditional | flops 273731584 | bytes 9695832 | solution.py:141
  131.0 1.6 fusion.24
  134.2 1.4 multiply_add_fusion.3
  136.3 1.8 %fusion.27 = f32[64,4,8,128]{3,2,0,1:T(8,128)S(1)} fusion(bf16[64,4,8,256]{3,0,2,1:T(8,128)(2,1)S(1)} %get-tuple-element.523, f32[64,4,8,128]{3,2,0,1:T(8,128)S(1)} %get-tuple-element.337, f32[64,4,8]{2,0,1:T(8,128)S(1)} %copy.47, bf16[256,4,128,1]{2,1,0,3:T(4,128)(2,1)} %bitcast.111), kind=kOutput, calls=%fused_computation.48 | convolution fusion | flops 134742016 | bytes 3416064 | tf_op jit(solution)/shard_map/while/body/eval_jaxpr/cond/branch_1_fun/qhgk,khd->qhgd/dot_general | solution.py:62
  144.5 1.5 collective-permute-start
  146.0 25.6 %collective-permute-done = bf16[1,128,4096]{2,1,0:T(8,128)(2,1)S(1)} collective-permute-done((bf16[1,128,4096]{2,1,0:T(8,128)(2,1)S(1)}, bf16[1,128,4096]{2,1,0:T(8,128)(2,1)S(1)}, u32[]{:S(2)}, u32[]{:S(2)}) %collective-permute-start) | collective-permute-done | bytes 1048608 | tf_op jit(solution)/shard_map/ppermute | solution.py:21
  (126 shorter events, 45.9 us)
Async XLA Ops:
  6.5 6.3 %copy-start.17 = (s32[1,4]{1,0:T(1,128)S(1)}, s32[1,4]{1,0:T(1,128)}, u32[]{:S(2)}) copy-start(s32[1,4]{1,0:T(1,128)} %param.19) | copy-start | bytes 52
  6.5 7.0 %copy-start.13 = (bf16[1,128,4096]{2,1,0:T(8,128)(2,1)S(1)}, bf16[1,128,4096]{2,1,0:T(8,128)(2,1)}, u32[]{:S(2)}) copy-start(bf16[1,128,4096]{2,1,0:T(8,128)(2,1)} %param.16) | copy-start | bytes 3145732
  6.5 31.9 %all-gather.4.cloned.1.call-start = ((), (), s32[]{:S(2)}) async-start(), calls=%async_computation | async-start | bytes 1179648 | tf_op jit(solution)/shard_map/all_gather | solution.py:152
  12.1 51.8 %all-gather.6.cloned.1.call-start = ((), (), s32[]{:S(2)}) async-start(), calls=%async_computation.1 | async-start | bytes 1179648 | tf_op jit(solution)/shard_map/all_gather | solution.py:153
  69.1 3.5 %copy-start.14 = (s32[4,64]{1,0:T(4,128)}, s32[4,64]{1,0:T(4,128)S(1)}, u32[]{:S(2)}) copy-start(s32[4,64]{1,0:T(4,128)S(1)} %get-tuple-element.701) | copy-start | bytes 3076 | tf_op jit(solution)/shard_map/while
  69.9 7.9 %copy-start.15 = (s32[4,64]{1,0:T(4,128)}, s32[4,64]{1,0:T(4,128)S(1)}, u32[]{:S(2)}) copy-start(s32[4,64]{1,0:T(4,128)S(1)} %get-tuple-element.700) | copy-start | bytes 3076 | tf_op jit(solution)/shard_map/while
  71.3 6.5 %copy-start.16 = (s32[256]{0:T(256)}, s32[256]{0:T(256)S(1)}, u32[]{:S(2)}) copy-start(s32[256]{0:T(256)S(1)} %get-tuple-element.702) | copy-start | bytes 3076 | tf_op jit(solution)/shard_map/while
  81.0 2.3 %copy-start.1 = (f32[64,4,8]{0,2,1:T(8,128)}, f32[64,4,8]{0,2,1:T(8,128)S(1)}, u32[]{:S(2)}) copy-start(f32[64,4,8]{0,2,1:T(8,128)S(1)} %max.10) | copy-start | bytes 24580 | tf_op jit(solution)/shard_map/while/body/eval_jaxpr/cond
  84.1 1.8 %copy-start.2 = (f32[64,4,8]{0,2,1:T(8,128)S(1)}, f32[64,4,8]{0,2,1:T(8,128)}, u32[]{:S(2)}) copy-start(f32[64,4,8]{0,2,1:T(8,128)} %copy-done.1) | copy-start | bytes 24580 | tf_op jit(solution)/shard_map/while/body/eval_jaxpr/cond
  91.7 2.3 %copy-start.3 = (f32[64,4,8]{0,2,1:T(8,128)}, f32[64,4,8]{0,2,1:T(8,128)S(1)}, u32[]{:S(2)}) copy-start(f32[64,4,8]{0,2,1:T(8,128)S(1)} %max.11) | copy-start | bytes 24580 | tf_op jit(solution)/shard_map/while/body/eval_jaxpr/cond
  94.8 1.8 %copy-start.4 = (f32[64,4,8]{0,2,1:T(8,128)S(1)}, f32[64,4,8]{0,2,1:T(8,128)}, u32[]{:S(2)}) copy-start(f32[64,4,8]{0,2,1:T(8,128)} %copy-done.3) | copy-start | bytes 24580 | tf_op jit(solution)/shard_map/while/body/eval_jaxpr/cond
  101.7 0.9 copy-start.9
  101.7 1.5 copy-start.5
  103.2 0.6 copy-start.10
  104.6 1.8 %copy-start.6 = (f32[64,4,8]{0,2,1:T(8,128)S(1)}, f32[64,4,8]{0,2,1:T(8,128)}, u32[]{:S(2)}) copy-start(f32[64,4,8]{0,2,1:T(8,128)} %copy-done.5) | copy-start | bytes 24580 | tf_op jit(solution)/shard_map/while/body/eval_jaxpr/cond
  110.6 3.5 %copy-start.14 = (s32[4,64]{1,0:T(4,128)}, s32[4,64]{1,0:T(4,128)S(1)}, u32[]{:S(2)}) copy-start(s32[4,64]{1,0:T(4,128)S(1)} %get-tuple-element.701) | copy-start | bytes 3076 | tf_op jit(solution)/shard_map/while
  111.4 7.9 %copy-start.15 = (s32[4,64]{1,0:T(4,128)}, s32[4,64]{1,0:T(4,128)S(1)}, u32[]{:S(2)}) copy-start(s32[4,64]{1,0:T(4,128)S(1)} %get-tuple-element.700) | copy-start | bytes 3076 | tf_op jit(solution)/shard_map/while
  112.8 6.5 %copy-start.16 = (s32[256]{0:T(256)}, s32[256]{0:T(256)S(1)}, u32[]{:S(2)}) copy-start(s32[256]{0:T(256)S(1)} %get-tuple-element.702) | copy-start | bytes 3076 | tf_op jit(solution)/shard_map/while
  122.5 2.3 %copy-start.1 = (f32[64,4,8]{0,2,1:T(8,128)}, f32[64,4,8]{0,2,1:T(8,128)S(1)}, u32[]{:S(2)}) copy-start(f32[64,4,8]{0,2,1:T(8,128)S(1)} %max.10) | copy-start | bytes 24580 | tf_op jit(solution)/shard_map/while/body/eval_jaxpr/cond
  125.6 1.8 %copy-start.2 = (f32[64,4,8]{0,2,1:T(8,128)S(1)}, f32[64,4,8]{0,2,1:T(8,128)}, u32[]{:S(2)}) copy-start(f32[64,4,8]{0,2,1:T(8,128)} %copy-done.1) | copy-start | bytes 24580 | tf_op jit(solution)/shard_map/while/body/eval_jaxpr/cond
  133.3 2.3 %copy-start.3 = (f32[64,4,8]{0,2,1:T(8,128)}, f32[64,4,8]{0,2,1:T(8,128)S(1)}, u32[]{:S(2)}) copy-start(f32[64,4,8]{0,2,1:T(8,128)S(1)} %max.11) | copy-start | bytes 24580 | tf_op jit(solution)/shard_map/while/body/eval_jaxpr/cond
  136.3 1.8 %copy-start.4 = (f32[64,4,8]{0,2,1:T(8,128)S(1)}, f32[64,4,8]{0,2,1:T(8,128)}, u32[]{:S(2)}) copy-start(f32[64,4,8]{0,2,1:T(8,128)} %copy-done.3) | copy-start | bytes 24580 | tf_op jit(solution)/shard_map/while/body/eval_jaxpr/cond
  144.5 27.2 %collective-permute-start = (bf16[1,128,4096]{2,1,0:T(8,128)(2,1)S(1)}, bf16[1,128,4096]{2,1,0:T(8,128)(2,1)S(1)}, u32[]{:S(2)}, u32[]{:S(2)}) collective-permute-start(bf16[1,128,4096]{2,1,0:T(8,128)(2,1)S(1)} %convert_element_type.99), channel_id=1, source_target_pairs={{3,0},{0,1},{1,2},{2,3},{7,4},{4,5},{5,6},{6,7},{11,8},{8,9},{9,10... | collective-permute-start | bytes 3145736 | tf_op jit(solution)/shard_map/ppermute | solution.py:21
Sparse Core Ops, SparseCore 0:
  12.2 26.1 all-gather.3
  40.3 23.4 all-gather.5
where the time goes:
time: 182 us; the launch traced here: 179 us
  waiting for transfers between devices  69.9 us (38%)
  other arithmetic  32.3 us (18%)
  local copies, waits for them, and re-layouts  31.3 us (17%)
  matrix products  17.2 us (9%)
  between operations  15 us (8%)
  loops' own time  12.1 us (7%)
    ppermute x1, waiting for transfers between devices, passed_along(): return lax.ppermute(block, axis, route)  25.6 us
    all_gather x1, waiting for transfers between devices, on_device(): value_fragment = lax.all_gather(value_rows, 'ctx', axis=0, tiled=True)  25.4 us
    all_gather x1, waiting for transfers between devices, on_device(): key_fragment = lax.all_gather(turned_keys, 'ctx', axis=0, tiled=True)  18.2 us
    another operation x1, loops' own time, on_device(): lax.scan(one_block, initial, (key_block_list, value_block_list, jnp.arang...  11.6 us
    dot_general x5, matrix products, absorb(): jnp.einsum('qhgk,khd->qhgd', weights.astype(jnp.bfloat16), value_part, pr...  9.14 us
    dot_general x5, matrix products, absorb(): jnp.einsum('qhgd,khd->qhgk', query_part, key_part, preferred_element_type...  8.1 us
    add x5, other arithmetic, absorb(): run_total = run_total * rescale + jnp.sum(weights, axis=-1)  6.03 us
    dynamic_slice x4, local copies, waits for them, and re-layouts, on_device(): lax.scan(one_block, initial, (key_block_list, value_block_list, jnp.arang...  5.08 us
  transfers between devices with their start and end apart: 3, of which 3 were waited for; matrix products, arithmetic and copies ran while one was open for 4% of the time, Pallas kernels for 0%

commit v1 on v0

v1 whole, which is shorter than its diff:
```python
from functools import partial
import math

import jax
import jax.numpy as jnp
from jax import lax
from jax.experimental import pallas as pl
from jax.experimental.pallas import tpu as pltpu
from jax.sharding import PartitionSpec as P

HEADS = 32
KV = 4
D = 128
GROUP = HEADS // KV
STACK = 4
SUBS = GROUP // STACK
THETA = 500000.0
MASKED = -1e30
SCALE = math.log2(math.e) / math.sqrt(D)
MESH = pl.DeviceIdType.MESH


def kernel(
    n, sections, q_ref, k_ref, v_ref, len_ref, num_ref, den_ref, out_ref,
    kv, cos_ref, sin_ref, bias_e, bias_l, obuf,
    send_sem, recv_sem, osend_sem, orecv_sem,
):
    me = lax.axis_index("ctx")
    sec = lax.axis_index("section")
    nxt = lax.rem(sec + 1, sections)
    prv = lax.rem(sec + sections - 1, sections)
    chips = n // 2
    chip, core = me // 2, me % 2
    partner = chip * 2 + 1 - core
    rows = q_ref.shape[1]
    half = rows // 2

    def peer(d):
        return lax.rem(chip + d, chips) * 2 + core

    barrier = pltpu.get_barrier_semaphore()
    for d in range(1, chips):
        pl.semaphore_signal(barrier, inc=1, device_id={"ctx": peer(d)}, device_id_type=MESH)
    pl.semaphore_signal(barrier, inc=1, device_id={"ctx": partner}, device_id_type=MESH)
    pl.semaphore_signal(barrier, inc=1, device_id={"section": nxt}, device_id_type=MESH)
    pl.semaphore_signal(barrier, inc=1, device_id={"section": prv}, device_id_type=MESH)

    r = lax.broadcasted_iota(jnp.int32, (rows, D), 0)
    pos = jnp.where(r < half, me * half + r, (2 * n - 1 - me) * half + r - half)
    start = jnp.zeros_like(pos)
    end = jnp.int32(0)
    for d in range(len_ref.shape[1]):
        length = len_ref[0, d]
        end = end + length
        start = start + jnp.where(pos >= end, length, 0)
    ratio = jnp.full((rows, D), num_ref[0], jnp.int32).astype(jnp.float32) / jnp.full(
        (rows, D), den_ref[0], jnp.int32
    ).astype(jnp.float32)
    lane = lax.broadcasted_iota(jnp.int32, (rows, D), 1)
    k_index = jnp.where(lane < D // 2, lane, lane - D // 2).astype(jnp.float32)
    freq = jnp.exp(k_index * (-2.0 / D * math.log(THETA)))
    angle = (pos - start).astype(jnp.float32) * ratio * freq
    cos = jnp.cos(angle)
    sin = jnp.where(lane < D // 2, -1.0, 1.0) * jnp.sin(angle)
    cos_ref[...] = cos
    sin_ref[...] = sin

    def rotate(x, c, s):
        x = x.astype(jnp.float32)
        return (x * c + pltpu.roll(x, D // 2, 1) * s).astype(jnp.bfloat16)

    def copy(h, shard, slot, to):
        return pltpu.make_async_remote_copy(
            src_ref=kv.at[h, shard],
            dst_ref=kv.at[h, shard],
            send_sem=send_sem.at[h, slot],
            recv_sem=recv_sem.at[h, shard],
            device_id={"ctx": to},
            device_id_type=MESH,
        )

    for h in range(KV):
        cols = slice(h * D, (h + 1) * D)
        kv[h, me, :, :D] = rotate(k_ref[0, :, cols], cos, sin)
        kv[h, me, :, D:] = v_ref[0, :, cols]
    pl.semaphore_wait(barrier, chips + 2)

    def push(h, _):
        for d in range(1, chips):
            copy(h, me, d, peer(d)).start()
        copy(h, me, 0, partner).start()
        return 0

    lax.fori_loop(0, KV, push, 0)

    def forward(h):
        for d in range(1, chips):
            shard = peer(chips - d)
            copy(h, shard, chips + d, partner).wait_recv()
            copy(h, shard, chips + d, partner).start()

    keys = n * half
    index = lax.broadcasted_iota(jnp.int32, (rows, keys), 1)
    q_pos, q_start = pos[:, :1], start[:, :1]
    bias_e[...] = jnp.where((index <= q_pos) & (index >= q_start), 0.0, MASKED)
    index = lax.broadcasted_iota(jnp.int32, (half, keys), 1)
    late = (2 * n - 1) * half + lax.rem(index, half) - lax.div(index, half) * half
    bias_l[...] = jnp.where((late <= q_pos[half:]) & (late >= q_start[half:]), 0.0, MASKED)

    forward(0)

    def out_copy(h, sub):
        cols = pl.ds(pl.multiple_of((h * SUBS + sub) * STACK * D, D), STACK * D)
        return pltpu.make_async_remote_copy(
            src_ref=obuf.at[:, cols],
            dst_ref=out_ref.at[0, :, cols],
            send_sem=osend_sem.at[h, sub],
            recv_sem=orecv_sem.at[h, sub],
            device_id={"section": nxt},
            device_id_type=MESH,
        )

    def attend(h, sub):
        c, s = cos_ref[...], sin_ref[...]
        base = (h * SUBS + sub) * STACK * D
        heads = [
            rotate(q_ref[0, :, pl.ds(pl.multiple_of(base + g * D, D), D)], c, s)
            for g in range(STACK)
        ]
        early_kv, late_kv = kv[h, :, :half, :], kv[h, :, half:, :]
        ke = early_kv[:, :, :D].reshape(keys, D)
        kl = late_kv[:, :, :D].reshape(keys, D)
        ones = jnp.ones((keys, D), jnp.bfloat16)
        ve = jnp.concatenate([early_kv[:, :, D:].reshape(keys, D), ones], axis=1)
        vl = jnp.concatenate([late_kv[:, :, D:].reshape(keys, D), ones], axis=1)
        dims = (((1,), (1,)), ((), ()))
        qa = jnp.concatenate(heads, axis=0)
        ql = jnp.concatenate([x[half:] for x in heads], axis=0)
        se = lax.dot_general(qa, ke, dims, preferred_element_type=jnp.float32)
        sl = lax.dot_general(ql, kl, dims, preferred_element_type=jnp.float32)
        se = se.reshape(STACK, rows, keys) + bias_e[...][None]
        sl = sl.reshape(STACK, half, keys) + bias_l[...][None]
        me_ = jnp.max(se, axis=-1, keepdims=True)
        ml = jnp.maximum(jnp.max(sl, axis=-1, keepdims=True), me_[:, half:])
        ma = jnp.concatenate([me_[:, :half], ml], axis=1)
        pe = jnp.exp2((se - ma) * SCALE).astype(jnp.bfloat16).reshape(STACK * rows, keys)
        pL = jnp.exp2((sl - ml) * SCALE).astype(jnp.bfloat16).reshape(STACK * half, keys)
        ae = jnp.dot(pe, ve, preferred_element_type=jnp.float32).reshape(STACK, rows, 2 * D)
        al = jnp.dot(pL, vl, preferred_element_type=jnp.float32).reshape(STACK, half, 2 * D)
        for g in range(STACK):
            cols = pl.ds(pl.multiple_of(base + g * D, D), D)
            top = ae[g, :half]
            low = ae[g, half:] + al[g]
            obuf[:half, cols] = (top[:, :D] / top[:, D:]).astype(jnp.bfloat16)
            obuf[half:, cols] = (low[:, :D] / low[:, D:]).astype(jnp.bfloat16)
        out_copy(h, sub).start()

    def head(h, _):
        for d in range(chips):
            shard = lax.rem(chip + d, chips) * 2 + 1 - core
            copy(h, shard, 0, partner).wait_recv()
        attend(h, 0)

        @pl.when(h + 1 < KV)
        def _():
            forward(h + 1)

        for sub in range(1, SUBS):
            attend(h, sub)
        return 0

    lax.fori_loop(0, KV, head, 0)

    def finish(h, _):
        for d in range(2 * chips):
            if d != chips:
                copy(h, me, d, partner).wait_send()
        for sub in range(SUBS):
            out_copy(h, sub).wait_send()
            out_copy(h, sub).wait_recv()
        return 0

    lax.fori_loop(0, KV, finish, 0)


def solution(mesh):
    n, sections = mesh.shape["ctx"], mesh.shape["section"]

    def on_device(queries, keys, values, doc_lengths, interp_num, interp_den):
        rows = queries.shape[1]
        half = rows // 2
        vmem = pl.BlockSpec(memory_space=pltpu.VMEM)
        smem = pl.BlockSpec(memory_space=pltpu.SMEM)
        return pl.pallas_call(
            partial(kernel, n, sections),
            out_shape=jax.ShapeDtypeStruct(queries.shape, jnp.bfloat16),
            in_specs=[vmem, vmem, vmem, smem, smem, smem],
            out_specs=pl.BlockSpec(memory_space=pl.ANY),
            scratch_shapes=[
                pltpu.VMEM((KV, n, rows, 2 * D), jnp.bfloat16),
                pltpu.VMEM((rows, D), jnp.float32),
                pltpu.VMEM((rows, D), jnp.float32),
                pltpu.VMEM((rows, n * half), jnp.float32),
                pltpu.VMEM((half, n * half), jnp.float32),
                pltpu.VMEM((rows, HEADS * D), jnp.bfloat16),
                pltpu.SemaphoreType.DMA((KV, n)),
                pltpu.SemaphoreType.DMA((KV, n)),
                pltpu.SemaphoreType.DMA((KV, SUBS)),
                pltpu.SemaphoreType.DMA((KV, SUBS)),
            ],
            compiler_params=pltpu.CompilerParams(
                collective_id=0, has_side_effects=True, vmem_limit_bytes=56 * 1024 * 1024
            ),
        )(queries, keys, values, doc_lengths, interp_num, interp_den)

    tokens = P("section", "ctx", None)
    return jax.shard_map(
        on_device,
        mesh=mesh,
        in_specs=(tokens, tokens, tokens, P("section", None), P(), P()),
        out_specs=tokens,
        check_vma=False,
    )
```

time: 182 us -> 43.9 us (0.24); the launches traced: 179 us -> 43.8 us
  waiting for transfers between devices: 69.9 us -> 0 us
  Pallas kernels: 0 us -> 40.2 us
  other arithmetic: 32.3 us -> 0 us
  local copies, waits for them, and re-layouts: 31.3 us -> 2.29 us
  matrix products: 17.2 us -> 0 us
  between operations: 15 us -> 1.3 us
  loops' own time: 12.1 us -> 0 us
    all_gather x2 -> x0, waiting for transfers between devices: 43.6 us -> none  [the longest x1 25.4 us: on_device(): value_fragment = lax.all_gather(value_rows, 'ctx', axis=0, tiled=True)]
    pallas_call x0 -> x1, Pallas kernels: none -> 40.2 us  [on_device(): pl.pallas_call(partial(kernel, n, sections), out_shape=jax.ShapeDtypeStru...]
    ppermute x1 -> x0, waiting for transfers between devices: 25.6 us -> none  [passed_along(): return lax.ppermute(block, axis, route)]
    dot_general x10 -> x0, matrix products: 17.2 us -> none  [the longest x5 9.14 us: absorb(): jnp.einsum('qhgk,khd->qhgd', weights.astype(jnp.bfloat16), value_part, pr...]
    another operation x9 -> x0, loops' own time: 12.1 us -> none  [the longest x1 11.6 us: on_device(): lax.scan(one_block, initial, (key_block_list, value_block_list, jnp.arang...]
    add x9 -> x0, other arithmetic: 9.01 us -> none  [the longest x5 6.03 us: absorb(): run_total = run_total * rescale + jnp.sum(weights, axis=-1)]
    slice x5 -> x0, local copies, waits for them, and re-layouts: 6.54 us -> none  [the longest x2 3.84 us: absorb_block(): reshaped_keys[:, neighbor_index]]
    dynamic_slice x4 -> x0, local copies, waits for them, and re-layouts: 5.08 us -> none  [on_device(): lax.scan(one_block, initial, (key_block_list, value_block_list, jnp.arang...]
  transfers between devices with their start and end apart: 3 -> 0, of which waited for: 3 -> 0; matrix products, arithmetic and copies ran while one was open for 4% -> 0% of each run, Pallas kernels for 0% -> 0%
where the time goes in v1:
time: 43.9 us; the launch traced here: 43.8 us
  Pallas kernels  40.2 us (92%)
  local copies, waits for them, and re-layouts  2.29 us (5%)
  between operations  1.3 us (3%)
    pallas_call x1, Pallas kernels, on_device(): pl.pallas_call(partial(kernel, n, sections), out_shape=jax.ShapeDtypeStru...  40.2 us
    unnamed x1, local copies, waits for them, and re-layouts  2.29 us

profile of v1, /device:TPU:0, one launch (start us, length us, event | category | flops | bytes accessed | tf_op | source)
XLA Modules:
  0.0 43.8 jit_solution(14945848433162366478)
XLA Ops:
  1.3 40.2 %shard_map.64 = bf16[1,128,4096]{2,1,0:T(8,128)(2,1)} custom-call(bf16[1,128,4096]{2,1,0:T(8,128)(2,1)} %q_ref.1, bf16[1,128,512]{2,1,0:T(8,128)(2,1)} %k_ref.1, bf16[1,128,512]{2,1,0:T(8,128)(2,1)} %v_ref.1, s32[1,4]{1,0:T(1,128)} %len_ref.1, s32[1]{0:T(128)S(6)} %copy.8.num_ref, s32[1]{0:T(128)S(6)} %copy.9.den_ref), custom_call_target="tpu_custom_call" | custom-call | tf_op jit(solution)/shard_map/pallas_call | solution.py:194
  41.5 2.3 %copy.10 = bf16[1,128,4096]{2,1,0:T(8,128)(2,1)} copy(bf16[1,128,4096]{2,1,0:T(8,128)(2,1)} %shard_map.64) | data formatting | bytes 2097152

commit v2 on v1

--- a/solution.py
+++ b/solution.py
@@ -21,9 +21,10 @@
 
 
 def kernel(
-    n, sections, q_ref, k_ref, v_ref, len_ref, num_ref, den_ref, out_ref,
+    n, sections, q_hbm, k_hbm, v_hbm, len_ref, num_ref, den_ref, out_ref,
     kv, cos_ref, sin_ref, bias_e, bias_l, obuf,
-    send_sem, recv_sem, osend_sem, orecv_sem,
+    qbuf, kbuf, vbuf, kv_give, q_give, q_take, len_give, len_take,
+    send_sem, recv_sem, osend_sem, orecv_sem, zsend_sem, zrecv_sem, load_sem, store_sem,
 ):
     me = lax.axis_index("ctx")
     sec = lax.axis_index("section")
@@ -32,8 +33,22 @@
     chips = n // 2
     chip, core = me // 2, me % 2
     partner = chip * 2 + 1 - core
-    rows = q_ref.shape[1]
+    rows = qbuf.shape[0]
     half = rows // 2
+    last = (KV - 1) * GROUP * D
+
+    loads = [
+        pltpu.make_async_copy(k_hbm.at[0], kbuf, load_sem.at[0]),
+        pltpu.make_async_copy(v_hbm.at[0], vbuf, load_sem.at[1]),
+        pltpu.make_async_copy(
+            q_hbm.at[0, :, last:], qbuf.at[:, last:], load_sem.at[2]
+        ),
+        pltpu.make_async_copy(
+            q_hbm.at[0, :, :last], qbuf.at[:, :last], load_sem.at[3]
+        ),
+    ]
+    for load in loads:
+        load.start()
 
     def peer(d):
         return lax.rem(chip + d, chips) * 2 + core
@@ -47,12 +62,18 @@
 
     r = lax.broadcasted_iota(jnp.int32, (rows, D), 0)
     pos = jnp.where(r < half, me * half + r, (2 * n - 1 - me) * half + r - half)
-    start = jnp.zeros_like(pos)
-    end = jnp.int32(0)
-    for d in range(len_ref.shape[1]):
-        length = len_ref[0, d]
-        end = end + length
-        start = start + jnp.where(pos >= end, length, 0)
+    def starts(lengths):
+        begin = jnp.zeros_like(pos)
+        end = jnp.zeros((1, D), jnp.int32)
+        for length in lengths:
+            end = end + length
+            begin = begin + jnp.where(pos >= end, length, 0)
+        return begin
+
+    docs = len_ref.shape[1]
+    for d in range(docs):
+        len_give[d : d + 1, :] = jnp.full((1, D), len_ref[0, d], jnp.int32)
+    start = starts([len_give[d : d + 1, :] for d in range(docs)])
     ratio = jnp.full((rows, D), num_ref[0], jnp.int32).astype(jnp.float32) / jnp.full(
         (rows, D), den_ref[0], jnp.int32
     ).astype(jnp.float32)
@@ -79,19 +100,49 @@
             device_id_type=MESH,
         )
 
-    for h in range(KV):
-        cols = slice(h * D, (h + 1) * D)
-        kv[h, me, :, :D] = rotate(k_ref[0, :, cols], cos, sin)
-        kv[h, me, :, D:] = v_ref[0, :, cols]
-    pl.semaphore_wait(barrier, chips + 2)
-
-    def push(h, _):
+    zpairs = [(kv_give, kv.at[KV - 1, me]), (len_give, len_take)]
+    for sub in range(SUBS):
+        zpairs.append((q_give.at[sub], q_take.at[sub]))
+    zcopies = [
+        pltpu.make_async_remote_copy(
+            src_ref=src,
+            dst_ref=dst,
+            send_sem=zsend_sem.at[i],
+            recv_sem=zrecv_sem.at[i],
+            device_id={"section": nxt},
+            device_id_type=MESH,
+        )
+        for i, (src, dst) in enumerate(zpairs)
+    ]
+
+    def push(h):
         for d in range(1, chips):
             copy(h, me, d, peer(d)).start()
         copy(h, me, 0, partner).start()
-        return 0
-
-    lax.fori_loop(0, KV, push, 0)
+
+    loads[0].wait()
+    loads[1].wait()
+    for h in range(KV):
+        cols = slice(h * D, (h + 1) * D)
+        turned = rotate(kbuf[:, cols], cos, sin)
+        if h == KV - 1:
+            kv_give[:, :D] = turned
+            kv_give[:, D:] = vbuf[:, cols]
+        else:
+            kv[h, me, :, :D] = turned
+            kv[h, me, :, D:] = vbuf[:, cols]
+    pl.semaphore_wait(barrier, chips + 2)
+    zcopies[0].start()
+    zcopies[1].start()
+    push(0)
+    loads[2].wait()
+    for sub in range(SUBS):
+        for g in range(STACK):
+            at = last + (sub * STACK + g) * D
+            q_give[sub, :, g * D : (g + 1) * D] = rotate(qbuf[:, at : at + D], cos, sin)
+        zcopies[2 + sub].start()
+    for h in range(1, KV - 1):
+        push(h)
 
     def forward(h):
         for d in range(1, chips):
@@ -100,13 +151,18 @@
             copy(h, shard, chips + d, partner).start()
 
     keys = n * half
-    index = lax.broadcasted_iota(jnp.int32, (rows, keys), 1)
-    q_pos, q_start = pos[:, :1], start[:, :1]
-    bias_e[...] = jnp.where((index <= q_pos) & (index >= q_start), 0.0, MASKED)
-    index = lax.broadcasted_iota(jnp.int32, (half, keys), 1)
-    late = (2 * n - 1) * half + lax.rem(index, half) - lax.div(index, half) * half
-    bias_l[...] = jnp.where((late <= q_pos[half:]) & (late >= q_start[half:]), 0.0, MASKED)
-
+
+    def set_bias(begin):
+        q_pos, q_start = pos[:, :1], begin[:, :1]
+        index = lax.broadcasted_iota(jnp.int32, (rows, keys), 1)
+        bias_e[...] = jnp.where((index <= q_pos) & (index >= q_start), 0.0, MASKED)
+        index = lax.broadcasted_iota(jnp.int32, (half, keys), 1)
+        late = (2 * n - 1) * half + lax.rem(index, half) - lax.div(index, half) * half
+        seen = (late <= q_pos[half:]) & (late >= q_start[half:])
+        bias_l[...] = jnp.where(seen, 0.0, MASKED)
+
+    set_bias(start)
+    loads[3].wait()
     forward(0)
 
     def out_copy(h, sub):
@@ -120,13 +176,16 @@
             device_id_type=MESH,
         )
 
-    def attend(h, sub):
+    def own_heads(h, sub):
         c, s = cos_ref[...], sin_ref[...]
         base = (h * SUBS + sub) * STACK * D
-        heads = [
-            rotate(q_ref[0, :, pl.ds(pl.multiple_of(base + g * D, D), D)], c, s)
+        return [
+            rotate(qbuf[:, pl.ds(pl.multiple_of(base + g * D, D), D)], c, s)
             for g in range(STACK)
         ]
+
+    def attend(h, sub, heads):
+        base = (h * SUBS + sub) * STACK * D
         early_kv, late_kv = kv[h, :, :half, :], kv[h, :, half:, :]
         ke = early_kv[:, :, :D].reshape(keys, D)
         kl = late_kv[:, :, :D].reshape(keys, D)
@@ -153,34 +212,63 @@
             low = ae[g, half:] + al[g]
             obuf[:half, cols] = (top[:, :D] / top[:, D:]).astype(jnp.bfloat16)
             obuf[half:, cols] = (low[:, :D] / low[:, D:]).astype(jnp.bfloat16)
-        out_copy(h, sub).start()
-
-    def head(h, _):
+
+    def from_partner(h):
         for d in range(chips):
             shard = lax.rem(chip + d, chips) * 2 + 1 - core
             copy(h, shard, 0, partner).wait_recv()
-        attend(h, 0)
-
-        @pl.when(h + 1 < KV)
+
+    def head(h, _):
+        from_partner(h)
+        attend(h, 0, own_heads(h, 0))
+        out_copy(h, 0).start()
+
+        @pl.when(h == 0)
         def _():
-            forward(h + 1)
-
+            zcopies[0].wait_recv()
+            push(KV - 1)
+
+        forward(h + 1)
         for sub in range(1, SUBS):
-            attend(h, sub)
+            attend(h, sub, own_heads(h, sub))
+            out_copy(h, sub).start()
         return 0
 
-    lax.fori_loop(0, KV, head, 0)
+    lax.fori_loop(0, KV - 1, head, 0)
+
+    zcopies[1].wait_recv()
+    set_bias(starts([len_take[d : d + 1, :] for d in range(docs)]))
+    from_partner(KV - 1)
+    stores = []
+    for sub in range(SUBS):
+        zcopies[2 + sub].wait_recv()
+        heads = [q_take[sub, :, g * D : (g + 1) * D] for g in range(STACK)]
+        attend(KV - 1, sub, heads)
+        at = last + sub * STACK * D
+        cols = slice(at, at + STACK * D)
+        store = pltpu.make_async_copy(obuf.at[:, cols], out_ref.at[0, :, cols], store_sem.at[sub])
+        store.start()
+        stores.append(store)
 
     def finish(h, _):
         for d in range(2 * chips):
             if d != chips:
                 copy(h, me, d, partner).wait_send()
+        return 0
+
+    lax.fori_loop(0, KV, finish, 0)
+    for store in stores:
+        store.wait()
+    for zcopy in zcopies:
+        zcopy.wait_send()
+
+    def arrive(h, _):
         for sub in range(SUBS):
             out_copy(h, sub).wait_send()
             out_copy(h, sub).wait_recv()
         return 0
 
-    lax.fori_loop(0, KV, finish, 0)
+    lax.fori_loop(0, KV - 1, arrive, 0)
 
 
 def solution(mesh):
@@ -189,12 +277,13 @@
     def on_device(queries, keys, values, doc_lengths, interp_num, interp_den):
         rows = queries.shape[1]
         half = rows // 2
-        vmem = pl.BlockSpec(memory_space=pltpu.VMEM)
+        docs = doc_lengths.shape[1]
+        hbm = pl.BlockSpec(memory_space=pltpu.HBM)
         smem = pl.BlockSpec(memory_space=pltpu.SMEM)
         return pl.pallas_call(
             partial(kernel, n, sections),
             out_shape=jax.ShapeDtypeStruct(queries.shape, jnp.bfloat16),
-            in_specs=[vmem, vmem, vmem, smem, smem, smem],
+            in_specs=[hbm, hbm, hbm, smem, smem, smem],
             out_specs=pl.BlockSpec(memory_space=pl.ANY),
             scratch_shapes=[
                 pltpu.VMEM((KV, n, rows, 2 * D), jnp.bfloat16),
@@ -203,13 +292,25 @@
                 pltpu.VMEM((rows, n * half), jnp.float32),
                 pltpu.VMEM((half, n * half), jnp.float32),
                 pltpu.VMEM((rows, HEADS * D), jnp.bfloat16),
+                pltpu.VMEM((rows, HEADS * D), jnp.bfloat16),
+                pltpu.VMEM((rows, KV * D), jnp.bfloat16),
+                pltpu.VMEM((rows, KV * D), jnp.bfloat16),
+                pltpu.VMEM((rows, 2 * D), jnp.bfloat16),
+                pltpu.VMEM((SUBS, rows, STACK * D), jnp.bfloat16),
+                pltpu.VMEM((SUBS, rows, STACK * D), jnp.bfloat16),
+                pltpu.VMEM((docs, D), jnp.int32),
+                pltpu.VMEM((docs, D), jnp.int32),
                 pltpu.SemaphoreType.DMA((KV, n)),
                 pltpu.SemaphoreType.DMA((KV, n)),
                 pltpu.SemaphoreType.DMA((KV, SUBS)),
                 pltpu.SemaphoreType.DMA((KV, SUBS)),
+                pltpu.SemaphoreType.DMA((2 + SUBS,)),
+                pltpu.SemaphoreType.DMA((2 + SUBS,)),
+                pltpu.SemaphoreType.DMA((4,)),
+                pltpu.SemaphoreType.DMA((SUBS,)),
             ],
             compiler_params=pltpu.CompilerParams(
-                collective_id=0, has_side_effects=True, vmem_limit_bytes=56 * 1024 * 1024
+                collective_id=0, has_side_effects=True, vmem_limit_bytes=(16 + n) * 1024 * 1024
             ),
         )(queries, keys, values, doc_lengths, interp_num, interp_den)
 

time: 43.9 us -> 39.7 us (0.904)
  Pallas kernels: 40.2 us -> 34.2 us
  local copies, waits for them, and re-layouts: 2.29 us -> 4 us
    pallas_call x1, Pallas kernels: 40.2 us -> 34.2 us  [on_device(): pl.pallas_call(partial(kernel, n, sections), out_shape=jax.ShapeDtypeStru...]
    unnamed x1 -> x9, local copies, waits for them, and re-layouts: 2.29 us -> 4 us
where the time goes in v2:
time: 39.7 us; the launch traced here: 39.5 us
  Pallas kernels  34.2 us (86%)
  local copies, waits for them, and re-layouts  4 us (10%)
  between operations  1.34 us (3%)
    pallas_call x1, Pallas kernels, on_device(): pl.pallas_call(partial(kernel, n, sections), out_shape=jax.ShapeDtypeStru...  34.2 us
    unnamed x9, local copies, waits for them, and re-layouts  4 us

profile of v2, /device:TPU:0, one launch (start us, length us, event | category | flops | bytes accessed | tf_op | source)
XLA Modules:
  0.0 39.5 jit_solution(10116163592649513017)
XLA Ops:
  0.7 0.0 copy-start.3
  1.3 0.0 copy-done.3
  1.3 0.0 copy-start
  1.3 1.2 %copy-done = bf16[1,128,4096]{2,1,0:T(8,128)(2,1)S(1)} copy-done((bf16[1,128,4096]{2,1,0:T(8,128)(2,1)S(1)}, bf16[1,128,4096]{2,1,0:T(8,128)(2,1)}, u32[]{:S(2)}) %copy-start) | copy-done | bytes 1048600
  2.6 0.0 copy-start.1
  2.6 0.9 %copy-done.1 = bf16[1,128,512]{2,1,0:T(8,128)(2,1)S(1)} copy-done((bf16[1,128,512]{2,1,0:T(8,128)(2,1)S(1)}, bf16[1,128,512]{2,1,0:T(8,128)(2,1)}, u32[]{:S(2)}) %copy-start.1) | copy-done | bytes 131096
  3.5 0.0 copy-start.2
  3.5 0.9 %copy-done.2 = bf16[1,128,512]{2,1,0:T(8,128)(2,1)S(1)} copy-done((bf16[1,128,512]{2,1,0:T(8,128)(2,1)S(1)}, bf16[1,128,512]{2,1,0:T(8,128)(2,1)}, u32[]{:S(2)}) %copy-start.2) | copy-done | bytes 131096
  4.4 34.2 %shard_map.64 = bf16[1,128,4096]{2,1,0:T(8,128)(2,1)S(1)} custom-call(bf16[1,128,4096]{2,1,0:T(8,128)(2,1)S(1)} %copy-done, bf16[1,128,512]{2,1,0:T(8,128)(2,1)S(1)} %copy-done.1, bf16[1,128,512]{2,1,0:T(8,128)(2,1)S(1)} %copy-done.2, s32[1,4]{1,0:T(1,128)S(1)} %copy-done.3, s32[1]{0:T(128)S(6)} %copy.8.num_ref, s32[1]{0:T(128)S(6)} %copy.9.den_ref), custom_call_target="tpu_custom_call" | custom-call | tf_op jit(solution)/shard_map/pallas_call | solution.py:283
  38.6 1.0 %copy.10 = bf16[1,128,4096]{2,1,0:T(8,128)(2,1)} copy(bf16[1,128,4096]{2,1,0:T(8,128)(2,1)S(1)} %shard_map.64) | data formatting | bytes 2097152
Async XLA Ops:
  0.7 0.7 %copy-start.3 = (s32[1,4]{1,0:T(1,128)S(1)}, s32[1,4]{1,0:T(1,128)}, u32[]{:S(2)}) copy-start(s32[1,4]{1,0:T(1,128)} %len_ref.1) | copy-start | bytes 52
  1.3 1.2 %copy-start = (bf16[1,128,4096]{2,1,0:T(8,128)(2,1)S(1)}, bf16[1,128,4096]{2,1,0:T(8,128)(2,1)}, u32[]{:S(2)}) copy-start(bf16[1,128,4096]{2,1,0:T(8,128)(2,1)} %q_hbm.1) | copy-start | bytes 3145732
  2.6 0.9 %copy-start.1 = (bf16[1,128,512]{2,1,0:T(8,128)(2,1)S(1)}, bf16[1,128,512]{2,1,0:T(8,128)(2,1)}, u32[]{:S(2)}) copy-start(bf16[1,128,512]{2,1,0:T(8,128)(2,1)} %k_hbm.1) | copy-start | bytes 393220
  3.5 0.9 %copy-start.2 = (bf16[1,128,512]{2,1,0:T(8,128)(2,1)S(1)}, bf16[1,128,512]{2,1,0:T(8,128)(2,1)}, u32[]{:S(2)}) copy-start(bf16[1,128,512]{2,1,0:T(8,128)(2,1)} %v_hbm.1) | copy-start | bytes 393220

commit v3 on v2

--- a/solution.py
+++ b/solution.py
@@ -282,7 +282,7 @@
         smem = pl.BlockSpec(memory_space=pltpu.SMEM)
         return pl.pallas_call(
             partial(kernel, n, sections),
-            out_shape=jax.ShapeDtypeStruct(queries.shape, jnp.bfloat16),
+            out_shape=pltpu.VMEM(queries.shape, jnp.bfloat16),
             in_specs=[hbm, hbm, hbm, smem, smem, smem],
             out_specs=pl.BlockSpec(memory_space=pl.ANY),
             scratch_shapes=[
@@ -310,7 +310,7 @@
                 pltpu.SemaphoreType.DMA((SUBS,)),
             ],
             compiler_params=pltpu.CompilerParams(
-                collective_id=0, has_side_effects=True, vmem_limit_bytes=(16 + n) * 1024 * 1024
+                collective_id=0, has_side_effects=True, vmem_limit_bytes=56*1024*1024
             ),
         )(queries, keys, values, doc_lengths, interp_num, interp_den)
 

time: 39.7 us -> 36.4 us (0.917)
  local copies, waits for them, and re-layouts: 4 us -> 0.97 us
    unnamed x9 -> x1, local copies, waits for them, and re-layouts: 4 us -> 0.97 us
where the time goes in v3:
time: 36.4 us; the launch traced here: 36.2 us
  Pallas kernels  34 us (93%)
  between operations  1.3 us (4%)
  local copies, waits for them, and re-layouts  0.97 us (3%)
    pallas_call x1, Pallas kernels, on_device(): pl.pallas_call(partial(kernel, n, sections), out_shape=pltpu.VMEM(queries...  34 us
    unnamed x1, local copies, waits for them, and re-layouts  0.97 us

profile of v3, /device:TPU:0, one launch (start us, length us, event | category | flops | bytes accessed | tf_op | source)
XLA Modules:
  0.0 36.2 jit_solution(17256450022731017518)
XLA Ops:
  1.3 34.0 %shard_map.64 = bf16[1,128,4096]{2,1,0:T(8,128)(2,1)S(1)} custom-call(bf16[1,128,4096]{2,1,0:T(8,128)(2,1)} %q_hbm.1, bf16[1,128,512]{2,1,0:T(8,128)(2,1)} %k_hbm.1, bf16[1,128,512]{2,1,0:T(8,128)(2,1)} %v_hbm.1, s32[1,4]{1,0:T(1,128)} %len_ref.1, s32[1]{0:T(128)S(6)} %copy.9.num_ref, s32[1]{0:T(128)S(6)} %copy.10.den_ref), custom_call_target="tpu_custom_call" | custom-call | tf_op jit(solution)/shard_map/pallas_call | solution.py:283
  35.3 1.0 %copy.8 = bf16[1,128,4096]{2,1,0:T(8,128)(2,1)} copy(bf16[1,128,4096]{2,1,0:T(8,128)(2,1)S(1)} %shard_map.64) | data formatting | bytes 2097152

commit v4 on v3

--- a/solution.py
+++ b/solution.py
@@ -23,7 +23,7 @@
 def kernel(
     n, sections, q_hbm, k_hbm, v_hbm, len_ref, num_ref, den_ref, out_ref,
     kv, cos_ref, sin_ref, bias_e, bias_l, obuf,
-    qbuf, kbuf, vbuf, kv_give, q_give, q_take, len_give, len_take,
+    qbuf, kbuf, vbuf, kv_give, q_take, len_give, len_take,
     send_sem, recv_sem, osend_sem, orecv_sem, zsend_sem, zrecv_sem, load_sem, store_sem,
 ):
     me = lax.axis_index("ctx")
@@ -41,10 +41,7 @@
         pltpu.make_async_copy(k_hbm.at[0], kbuf, load_sem.at[0]),
         pltpu.make_async_copy(v_hbm.at[0], vbuf, load_sem.at[1]),
         pltpu.make_async_copy(
-            q_hbm.at[0, :, last:], qbuf.at[:, last:], load_sem.at[2]
-        ),
-        pltpu.make_async_copy(
-            q_hbm.at[0, :, :last], qbuf.at[:, :last], load_sem.at[3]
+            q_hbm.at[0, :, :last], qbuf.at[:, :last], load_sem.at[2]
         ),
     ]
     for load in loads:
@@ -60,49 +57,10 @@
     pl.semaphore_signal(barrier, inc=1, device_id={"section": nxt}, device_id_type=MESH)
     pl.semaphore_signal(barrier, inc=1, device_id={"section": prv}, device_id_type=MESH)
 
-    r = lax.broadcasted_iota(jnp.int32, (rows, D), 0)
-    pos = jnp.where(r < half, me * half + r, (2 * n - 1 - me) * half + r - half)
-    def starts(lengths):
-        begin = jnp.zeros_like(pos)
-        end = jnp.zeros((1, D), jnp.int32)
-        for length in lengths:
-            end = end + length
-            begin = begin + jnp.where(pos >= end, length, 0)
-        return begin
-
-    docs = len_ref.shape[1]
-    for d in range(docs):
-        len_give[d : d + 1, :] = jnp.full((1, D), len_ref[0, d], jnp.int32)
-    start = starts([len_give[d : d + 1, :] for d in range(docs)])
-    ratio = jnp.full((rows, D), num_ref[0], jnp.int32).astype(jnp.float32) / jnp.full(
-        (rows, D), den_ref[0], jnp.int32
-    ).astype(jnp.float32)
-    lane = lax.broadcasted_iota(jnp.int32, (rows, D), 1)
-    k_index = jnp.where(lane < D // 2, lane, lane - D // 2).astype(jnp.float32)
-    freq = jnp.exp(k_index * (-2.0 / D * math.log(THETA)))
-    angle = (pos - start).astype(jnp.float32) * ratio * freq
-    cos = jnp.cos(angle)
-    sin = jnp.where(lane < D // 2, -1.0, 1.0) * jnp.sin(angle)
-    cos_ref[...] = cos
-    sin_ref[...] = sin
-
-    def rotate(x, c, s):
-        x = x.astype(jnp.float32)
-        return (x * c + pltpu.roll(x, D // 2, 1) * s).astype(jnp.bfloat16)
-
-    def copy(h, shard, slot, to):
-        return pltpu.make_async_remote_copy(
-            src_ref=kv.at[h, shard],
-            dst_ref=kv.at[h, shard],
-            send_sem=send_sem.at[h, slot],
-            recv_sem=recv_sem.at[h, shard],
-            device_id={"ctx": to},
-            device_id_type=MESH,
-        )
-
     zpairs = [(kv_give, kv.at[KV - 1, me]), (len_give, len_take)]
     for sub in range(SUBS):
-        zpairs.append((q_give.at[sub], q_take.at[sub]))
+        at = last + sub * STACK * D
+        zpairs.append((q_hbm.at[0, :, at : at + STACK * D], q_take.at[sub]))
     zcopies = [
         pltpu.make_async_remote_copy(
             src_ref=src,
@@ -115,6 +73,52 @@
         for i, (src, dst) in enumerate(zpairs)
     ]
 
+    pl.semaphore_wait(barrier, chips + 2)
+    for sub in range(SUBS):
+        zcopies[2 + sub].start()
+
+    r = lax.broadcasted_iota(jnp.int32, (rows, D), 0)
+    pos = jnp.where(r < half, me * half + r, (2 * n - 1 - me) * half + r - half)
+    def starts(lengths):
+        begin = jnp.zeros_like(pos)
+        end = jnp.zeros((1, D), jnp.int32)
+        for length in lengths:
+            end = end + length
+            begin = begin + jnp.where(pos >= end, length, 0)
+        return begin
+
+    docs = len_ref.shape[1]
+    for d in range(docs):
+        len_give[d : d + 1, :] = jnp.full((1, D), len_ref[0, d], jnp.int32)
+    start = starts([len_give[d : d + 1, :] for d in range(docs)])
+    ratio = jnp.full((rows, D), num_ref[0], jnp.int32).astype(jnp.float32) / jnp.full(
+        (rows, D), den_ref[0], jnp.int32
+    ).astype(jnp.float32)
+    lane = lax.broadcasted_iota(jnp.int32, (rows, D), 1)
+    k_index = jnp.where(lane < D // 2, lane, lane - D // 2).astype(jnp.float32)
+    freq = jnp.exp(k_index * (-2.0 / D * math.log(THETA)))
+    def tables(begin):
+        angle = (pos - begin).astype(jnp.float32) * ratio * freq
+        return jnp.cos(angle), jnp.where(lane < D // 2, -1.0, 1.0) * jnp.sin(angle)
+
+    cos, sin = tables(start)
+    cos_ref[...] = cos
+    sin_ref[...] = sin
+
+    def rotate(x, c, s):
+        x = x.astype(jnp.float32)
+        return (x * c + pltpu.roll(x, D // 2, 1) * s).astype(jnp.bfloat16)
+
+    def copy(h, shard, slot, to):
+        return pltpu.make_async_remote_copy(
+            src_ref=kv.at[h, shard],
+            dst_ref=kv.at[h, shard],
+            send_sem=send_sem.at[h, slot],
+            recv_sem=recv_sem.at[h, shard],
+            device_id={"ctx": to},
+            device_id_type=MESH,
+        )
+
     def push(h):
         for d in range(1, chips):
             copy(h, me, d, peer(d)).start()
@@ -131,16 +135,9 @@
         else:
             kv[h, me, :, :D] = turned
             kv[h, me, :, D:] = vbuf[:, cols]
-    pl.semaphore_wait(barrier, chips + 2)
     zcopies[0].start()
     zcopies[1].start()
     push(0)
-    loads[2].wait()
-    for sub in range(SUBS):
-        for g in range(STACK):
-            at = last + (sub * STACK + g) * D
-            q_give[sub, :, g * D : (g + 1) * D] = rotate(qbuf[:, at : at + D], cos, sin)
-        zcopies[2 + sub].start()
     for h in range(1, KV - 1):
         push(h)
 
@@ -162,7 +159,7 @@
         bias_l[...] = jnp.where(seen, 0.0, MASKED)
 
     set_bias(start)
-    loads[3].wait()
+    loads[2].wait()
     forward(0)
 
     def out_copy(h, sub):
@@ -223,7 +220,7 @@
         attend(h, 0, own_heads(h, 0))
         out_copy(h, 0).start()
 
-        @pl.when(h == 0)
+        @pl.when(h == 1)
         def _():
             zcopies[0].wait_recv()
             push(KV - 1)
@@ -237,12 +234,16 @@
     lax.fori_loop(0, KV - 1, head, 0)
 
     zcopies[1].wait_recv()
-    set_bias(starts([len_take[d : d + 1, :] for d in range(docs)]))
+    begin = starts([len_take[d : d + 1, :] for d in range(docs)])
+    set_bias(begin)
+    cos, sin = tables(begin)
     from_partner(KV - 1)
     stores = []
     for sub in range(SUBS):
         zcopies[2 + sub].wait_recv()
-        heads = [q_take[sub, :, g * D : (g + 1) * D] for g in range(STACK)]
+        heads = [
+            rotate(q_take[sub, :, g * D : (g + 1) * D], cos, sin) for g in range(STACK)
+        ]
         attend(KV - 1, sub, heads)
         at = last + sub * STACK * D
         cols = slice(at, at + STACK * D)
@@ -297,7 +298,6 @@
                 pltpu.VMEM((rows, KV * D), jnp.bfloat16),
                 pltpu.VMEM((rows, 2 * D), jnp.bfloat16),
                 pltpu.VMEM((SUBS, rows, STACK * D), jnp.bfloat16),
-                pltpu.VMEM((SUBS, rows, STACK * D), jnp.bfloat16),
                 pltpu.VMEM((docs, D), jnp.int32),
                 pltpu.VMEM((docs, D), jnp.int32),
                 pltpu.SemaphoreType.DMA((KV, n)),
@@ -306,7 +306,7 @@
                 pltpu.SemaphoreType.DMA((KV, SUBS)),
                 pltpu.SemaphoreType.DMA((2 + SUBS,)),
                 pltpu.SemaphoreType.DMA((2 + SUBS,)),
-                pltpu.SemaphoreType.DMA((4,)),
+                pltpu.SemaphoreType.DMA((3,)),
                 pltpu.SemaphoreType.DMA((SUBS,)),
             ],
             compiler_params=pltpu.CompilerParams(

time: 36.4 us -> 36.7 us (level)
  no operation moved by 1% of the time
where the time goes in v4:
time: 36.7 us; the launch traced here: 36.5 us
  Pallas kernels  34.2 us (93%)
  between operations  1.3 us (4%)
  local copies, waits for them, and re-layouts  0.97 us (3%)
    pallas_call x1, Pallas kernels, on_device(): pl.pallas_call(partial(kernel, n, sections), out_shape=pltpu.VMEM(queries...  34.2 us
    unnamed x1, local copies, waits for them, and re-layouts  0.97 us

profile of v4, /device:TPU:0, one launch (start us, length us, event | category | flops | bytes accessed | tf_op | source)
XLA Modules:
  0.0 36.5 jit_solution(16583865446342301138)
XLA Ops:
  1.3 34.2 %shard_map.64 = bf16[1,128,4096]{2,1,0:T(8,128)(2,1)S(1)} custom-call(bf16[1,128,4096]{2,1,0:T(8,128)(2,1)} %q_hbm.1, bf16[1,128,512]{2,1,0:T(8,128)(2,1)} %k_hbm.1, bf16[1,128,512]{2,1,0:T(8,128)(2,1)} %v_hbm.1, s32[1,4]{1,0:T(1,128)} %len_ref.1, s32[1]{0:T(128)S(6)} %copy.9.num_ref, s32[1]{0:T(128)S(6)} %copy.10.den_ref), custom_call_target="tpu_custom_call" | custom-call | tf_op jit(solution)/shard_map/pallas_call | solution.py:284
  35.5 1.0 %copy.8 = bf16[1,128,4096]{2,1,0:T(8,128)(2,1)} copy(bf16[1,128,4096]{2,1,0:T(8,128)(2,1)S(1)} %shard_map.64) | data formatting | bytes 2097152
